TPU v7x, 128 devices: a whole 4x4x4 slice. The times are simulated.
128 devices in a mesh: rows: 16 (over x, y), store: 8 (over z, core).
Axes of the slice: x: 4, y: 4, z: 4, core: 2. Of those that a mesh axis runs over, the one named last changes fastest.
Arguments:
- stored: float32 [128, 1048576], P('store', 'rows'), as said below
- snap_slot: int32 [64], replicated, may hold values from 0 to 127, as said below
Outputs:
- modes: float32 [64, 1048576], P(None, ('rows', 'store'))
- factor: float32 [64, 64], replicated
Inputs may be any that keep to these rules, and one draw needn't show every extreme that they name: `snap_slot`: the numbers are distinct slots; slots s * 16 to (s + 1) * 16 - 1 belong to storage owner s. Owners hold uneven numbers of the panel's snapshots; one owner holds exactly 16 of them. `stored`: entries are finite; the panel has full rank.
All inputs are finite; a program needn't handle non-finite values.
Results may differ from a plain program's by a relative error of at most 0.0003.
Values sent between devices are 32-bit elements; how exact they have to be, the bound alone decides.
No kernel may reach another device: no remote copies, remote signals or barrier semaphores. Data moves between devices by JAX's collectives and lax.ppermute only.
A program may use at most 128 MiB of HBM per device.

v0:
```python
import math

import jax
import jax.numpy as jnp
from jax import lax
from jax.experimental import pallas as pl
from jax.experimental.pallas import tpu as pltpu
from jax.sharding import PartitionSpec as P

HIGHEST = lax.Precision.HIGHEST


def dot(a, b):
    return jnp.dot(a, b, precision=HIGHEST, preferred_element_type=jnp.float32)


def neighbour_sum(value):
    for axis, masks in (("store", (1, 2, 6)), ("rows", (1, 3, 4, 12))):
        for mask in masks:
            pairs = [(i, i ^ mask) for i in range(lax.axis_size(axis))]
            value = value + lax.ppermute(value, axis, pairs)
    return value


def eliminate(gram):
    n = gram.shape[0]
    rows = lax.broadcasted_iota(jnp.int32, (n, n), 0)
    columns = lax.broadcasted_iota(jnp.int32, (n, n), 1)
    whole = jnp.concatenate([gram, (rows == columns).astype(jnp.float32)], axis=1)
    below = lax.broadcasted_iota(jnp.int32, (8, 1), 0)
    blocks = [whole[8 * i : 8 * i + 8] for i in range(n // 8)]
    scales = []
    for j in range(n):
        b, s = divmod(j, 8)
        row = blocks[b][s : s + 1]
        pivot = row[:, j : j + 1]
        scales.append(lax.rsqrt(pivot))
        scaled = row / pivot
        for i in range(b, n // 8):
            column = blocks[i][:, j : j + 1]
            if i == b:
                column = jnp.where(below > s, column, 0.0)
            blocks[i] = blocks[i] - column * scaled
    diagonal = jnp.concatenate(
        [blocks[j // 8][j % 8 : j % 8 + 1, j : j + 1] for j in range(n)], axis=0
    )
    scale = jnp.concatenate(scales, axis=0)
    scale = scale * (1.5 - 0.5 * diagonal * scale * scale)
    whole = jnp.concatenate(blocks, axis=0) * scale
    upper = jnp.where(rows <= columns, whole[:, :n], 0.0)
    lower = jnp.where(rows >= columns, whole[:, n:], 0.0)
    return upper, lower


def factor_kernel(gram_ref, upper_ref, lower_ref):
    upper, lower = eliminate(gram_ref[...])
    upper_ref[...] = upper
    lower_ref[...] = lower


def factor_of(gram):
    shape = jax.ShapeDtypeStruct(gram.shape, jnp.float32)
    return pl.pallas_call(factor_kernel, out_shape=(shape, shape))(gram)


def per_device(stored, snap_slot):
    received = lax.all_to_all(stored, "store", split_axis=1, concat_axis=0, tiled=True)
    places = jnp.arange(received.shape[0], dtype=jnp.int32)
    selector = (snap_slot[:, None] == places[None, :]).astype(jnp.float32)
    panel = dot(selector, received)
    r_first, inverse_first = factor_of(neighbour_sum(dot(panel, panel.T)))
    basis = dot(inverse_first, panel)
    r_second, inverse_second = factor_of(neighbour_sum(dot(basis, basis.T)))
    scale = math.sqrt(panel.shape[1] * lax.axis_size(("rows", "store")))
    modes = dot(inverse_second * scale, basis)
    factor = dot(r_second, r_first) / scale
    return (modes, factor)


def solution(mesh):
    in_specs = (P("store", "rows"), P())
    out_specs = (P(None, ("rows", "store")), P())
    return jax.shard_map(
        per_device, mesh=mesh, in_specs=in_specs, out_specs=out_specs, check_vma=False
    )
```

profile of v0, /device:TPU:0, one launch (start us, length us, event | category | flops | bytes accessed | tf_op | source)
XLA Modules:
  0.0 144.4 jit_solution(2804742243018185215)
XLA Ops:
  0.6 2.5 %copy.8 = f32[2,8,8,8192]{3,2,0,1:T(8,128)S(1)} copy(f32[2,8,8,8192]{3,2,1,0:T(8,128)} %bitcast.19) | data formatting | bytes 8388608 | tf_op jit(solution)/shard_map/all_to_all | solution.py:67
  3.1 0.0 copy-start.3
  3.1 55.5 %all_to_all.19 = f32[16,8,8192]{2,0,1:T(8,128)S(1)} all-to-all(f32[16,8,8192]{2,0,1:T(8,128)S(1)} %bitcast.18), channel_id=1, replica_groups=mesh['rows'=16,'store'=8] {'store'}, dimensions={1} | all-to-all | bytes 8388608 | tf_op jit(solution)/shard_map/all_to_all | solution.py:67
  58.7 0.0 copy-done.3
  58.7 1.7 %fusion.2 = f32[64,8192]{1,0:T(8,128)S(1)} fusion(f32[128,8192]{1,0:T(8,128)S(1)} %bitcast.17, s32[64]{0:T(128)S(1)} %copy-done.3), kind=kOutput, calls=%fused_computation.5 | convolution fusion | flops 805314560 | bytes 6291712 | tf_op jit(solution)/shard_map/dot_general | solution.py:14
  60.4 1.8 %fusion.6 = f32[64,64]{1,0:T(8,128)S(1)} fusion(f32[64,8192]{1,0:T(8,128)S(1)} %fusion.2), kind=kOutput, calls=%fused_computation.9 | convolution fusion | flops 402653184 | bytes 2113536 | tf_op jit(solution)/shard_map/dot_general | solution.py:14
  62.2 0.1 collective-permute-start
  62.3 1.2 collective-permute-done
  63.5 0.6 collective-permute-start.1
  64.1 3.3 %collective-permute-done.1 = f32[64,64]{1,0:T(8,128)S(1)} collective-permute-done((f32[64,64]{1,0:T(8,128)S(1)}, f32[64,64]{1,0:T(8,128)S(1)}, u32[]{:S(2)}, u32[]{:S(2)}) %collective-permute-start.1) | collective-permute-done | bytes 16416 | tf_op jit(solution)/shard_map/ppermute | solution.py:21
  67.4 1.1 collective-permute-start.2
  68.5 4.0 %collective-permute-done.2 = f32[64,64]{1,0:T(8,128)S(1)} collective-permute-done((f32[64,64]{1,0:T(8,128)S(1)}, f32[64,64]{1,0:T(8,128)S(1)}, u32[]{:S(2)}, u32[]{:S(2)}) %collective-permute-start.2) | collective-permute-done | bytes 16416 | tf_op jit(solution)/shard_map/ppermute | solution.py:21
  72.5 1.6 %collective-permute-start.3 = (f32[64,64]{1,0:T(8,128)S(1)}, f32[64,64]{1,0:T(8,128)S(1)}, u32[]{:S(2)}, u32[]{:S(2)}) collective-permute-start(f32[64,64]{1,0:T(8,128)S(1)} %add.44), channel_id=1, source_target_pairs={{0,8},{8,0},{16,24},{24,16},{32,40},{40,32},{48,56},{56,48},{64,72... | collective-permute-start | bytes 49160 | tf_op jit(solution)/shard_map/ppermute | solution.py:21
  74.1 2.3 %collective-permute-done.3 = f32[64,64]{1,0:T(8,128)S(1)} collective-permute-done((f32[64,64]{1,0:T(8,128)S(1)}, f32[64,64]{1,0:T(8,128)S(1)}, u32[]{:S(2)}, u32[]{:S(2)}) %collective-permute-start.3) | collective-permute-done | bytes 16416 | tf_op jit(solution)/shard_map/ppermute | solution.py:21
  76.5 3.0 %collective-permute-start.4 = (f32[64,64]{1,0:T(8,128)S(1)}, f32[64,64]{1,0:T(8,128)S(1)}, u32[]{:S(2)}, u32[]{:S(2)}) collective-permute-start(f32[64,64]{1,0:T(8,128)S(1)} %add.45), channel_id=1, source_target_pairs={{0,24},{8,16},{16,8},{24,0},{32,56},{40,48},{48,40},{56,32},{64,88... | collective-permute-start | bytes 49160 | tf_op jit(solution)/shard_map/ppermute | solution.py:21
  79.5 2.1 %collective-permute-done.4 = f32[64,64]{1,0:T(8,128)S(1)} collective-permute-done((f32[64,64]{1,0:T(8,128)S(1)}, f32[64,64]{1,0:T(8,128)S(1)}, u32[]{:S(2)}, u32[]{:S(2)}) %collective-permute-start.4) | collective-permute-done | bytes 16416 | tf_op jit(solution)/shard_map/ppermute | solution.py:21
  81.6 1.5 %collective-permute-start.5 = (f32[64,64]{1,0:T(8,128)S(1)}, f32[64,64]{1,0:T(8,128)S(1)}, u32[]{:S(2)}, u32[]{:S(2)}) collective-permute-start(f32[64,64]{1,0:T(8,128)S(1)} %add.46), channel_id=1, source_target_pairs={{0,32},{8,40},{16,48},{24,56},{32,0},{40,8},{48,16},{56,24},{64,96... | collective-permute-start | bytes 49160 | tf_op jit(solution)/shard_map/ppermute | solution.py:21
  83.1 2.4 %collective-permute-done.5 = f32[64,64]{1,0:T(8,128)S(1)} collective-permute-done((f32[64,64]{1,0:T(8,128)S(1)}, f32[64,64]{1,0:T(8,128)S(1)}, u32[]{:S(2)}, u32[]{:S(2)}) %collective-permute-start.5) | collective-permute-done | bytes 16416 | tf_op jit(solution)/shard_map/ppermute | solution.py:21
  85.5 2.8 %collective-permute-start.6 = (f32[64,64]{1,0:T(8,128)S(1)}, f32[64,64]{1,0:T(8,128)S(1)}, u32[]{:S(2)}, u32[]{:S(2)}) collective-permute-start(f32[64,64]{1,0:T(8,128)S(1)} %add.47), channel_id=1, source_target_pairs={{0,96},{8,104},{16,112},{24,120},{32,64},{40,72},{48,80},{56,88},{... | collective-permute-start | bytes 49160 | tf_op jit(solution)/shard_map/ppermute | solution.py:21
  88.3 2.4 %collective-permute-done.6 = f32[64,64]{1,0:T(8,128)S(1)} collective-permute-done((f32[64,64]{1,0:T(8,128)S(1)}, f32[64,64]{1,0:T(8,128)S(1)}, u32[]{:S(2)}, u32[]{:S(2)}) %collective-permute-start.6) | collective-permute-done | bytes 16416 | tf_op jit(solution)/shard_map/ppermute | solution.py:21
  90.6 0.6 add.48.gram_ref
  91.3 7.0 %shard_map.41 = (f32[64,64]{1,0:T(8,128)}, f32[64,64]{1,0:T(8,128)}) custom-call(f32[64,64]{1,0:T(8,128)} %add.48.gram_ref), custom_call_target="tpu_custom_call" | custom-call | tf_op jit(solution)/shard_map/pallas_call | solution.py:63
  98.2 2.7 %fusion.7 = f32[64,8192]{1,0:T(8,128)S(1)} fusion(f32[64,64]{1,0:T(8,128)} %get-tuple-element.6, f32[64,8192]{1,0:T(8,128)S(1)} %fusion.2), kind=kOutput, calls=%fused_computation.10 | convolution fusion | flops 402653184 | bytes 4210688 | tf_op jit(solution)/shard_map/dot_general | solution.py:14
  100.9 0.0 copy-start
  100.9 1.8 %fusion.8 = f32[64,64]{1,0:T(8,128)S(1)} fusion(f32[64,8192]{1,0:T(8,128)S(1)} %fusion.7), kind=kOutput, calls=%fused_computation.11 | convolution fusion | flops 402653184 | bytes 2113536 | tf_op jit(solution)/shard_map/dot_general | solution.py:14
  102.7 0.0 copy-done
  102.7 0.1 collective-permute-start.7
  102.8 1.2 collective-permute-done.7
  104.0 0.0 collective-permute-start.8
  104.0 3.9 %collective-permute-done.8 = f32[64,64]{1,0:T(8,128)S(1)} collective-permute-done((f32[64,64]{1,0:T(8,128)S(1)}, f32[64,64]{1,0:T(8,128)S(1)}, u32[]{:S(2)}, u32[]{:S(2)}) %collective-permute-start.8) | collective-permute-done | bytes 16416 | tf_op jit(solution)/shard_map/ppermute | solution.py:21
  108.0 1.1 collective-permute-start.9
  109.1 4.0 %collective-permute-done.9 = f32[64,64]{1,0:T(8,128)S(1)} collective-permute-done((f32[64,64]{1,0:T(8,128)S(1)}, f32[64,64]{1,0:T(8,128)S(1)}, u32[]{:S(2)}, u32[]{:S(2)}) %collective-permute-start.9) | collective-permute-done | bytes 16416 | tf_op jit(solution)/shard_map/ppermute | solution.py:21
  113.1 0.4 collective-permute-start.10
  113.4 3.6 %collective-permute-done.10 = f32[64,64]{1,0:T(8,128)S(1)} collective-permute-done((f32[64,64]{1,0:T(8,128)S(1)}, f32[64,64]{1,0:T(8,128)S(1)}, u32[]{:S(2)}, u32[]{:S(2)}) %collective-permute-start.10) | collective-permute-done | bytes 16416 | tf_op jit(solution)/shard_map/ppermute | solution.py:21
  117.0 3.0 %collective-permute-start.11 = (f32[64,64]{1,0:T(8,128)S(1)}, f32[64,64]{1,0:T(8,128)S(1)}, u32[]{:S(2)}, u32[]{:S(2)}) collective-permute-start(f32[64,64]{1,0:T(8,128)S(1)} %add.52), channel_id=1, source_target_pairs={{0,24},{8,16},{16,8},{24,0},{32,56},{40,48},{48,40},{56,32},{64,88... | collective-permute-start | bytes 49160 | tf_op jit(solution)/shard_map/ppermute | solution.py:21
  120.0 2.1 %collective-permute-done.11 = f32[64,64]{1,0:T(8,128)S(1)} collective-permute-done((f32[64,64]{1,0:T(8,128)S(1)}, f32[64,64]{1,0:T(8,128)S(1)}, u32[]{:S(2)}, u32[]{:S(2)}) %collective-permute-start.11) | collective-permute-done | bytes 16416 | tf_op jit(solution)/shard_map/ppermute | solution.py:21
  122.1 0.3 collective-permute-start.12
  122.4 3.6 %collective-permute-done.12 = f32[64,64]{1,0:T(8,128)S(1)} collective-permute-done((f32[64,64]{1,0:T(8,128)S(1)}, f32[64,64]{1,0:T(8,128)S(1)}, u32[]{:S(2)}, u32[]{:S(2)}) %collective-permute-start.12) | collective-permute-done | bytes 16416 | tf_op jit(solution)/shard_map/ppermute | solution.py:21
  126.1 2.8 %collective-permute-start.13 = (f32[64,64]{1,0:T(8,128)S(1)}, f32[64,64]{1,0:T(8,128)S(1)}, u32[]{:S(2)}, u32[]{:S(2)}) collective-permute-start(f32[64,64]{1,0:T(8,128)S(1)} %add.54), channel_id=1, source_target_pairs={{0,96},{8,104},{16,112},{24,120},{32,64},{40,72},{48,80},{56,88},{... | collective-permute-start | bytes 49160 | tf_op jit(solution)/shard_map/ppermute | solution.py:21
  128.8 2.4 %collective-permute-done.13 = f32[64,64]{1,0:T(8,128)S(1)} collective-permute-done((f32[64,64]{1,0:T(8,128)S(1)}, f32[64,64]{1,0:T(8,128)S(1)}, u32[]{:S(2)}, u32[]{:S(2)}) %collective-permute-start.13) | collective-permute-done | bytes 16416 | tf_op jit(solution)/shard_map/ppermute | solution.py:21
  131.2 0.6 add.55.gram_ref
  131.8 6.9 %shard_map.42 = (f32[64,64]{1,0:T(8,128)}, f32[64,64]{1,0:T(8,128)}) custom-call(f32[64,64]{1,0:T(8,128)} %add.55.gram_ref), custom_call_target="tpu_custom_call" | custom-call | tf_op jit(solution)/shard_map/pallas_call | solution.py:63
  138.7 0.0 copy-start.1
  138.7 0.0 copy-start.2
  138.7 4.8 %fusion = f32[64,8192]{1,0:T(8,128)} fusion(f32[64,8192]{1,0:T(8,128)} %copy-done, f32[64,64]{1,0:T(8,128)} %get-tuple-element.7), kind=kOutput, calls=%fused_computation.2 | convolution fusion | flops 402657280 | bytes 4210688 | tf_op jit(solution)/shard_map/dot_general | solution.py:14
  143.6 0.0 copy-done.1
  143.6 0.0 copy-done.2
  143.6 0.8 convolution_multiply_fusion
  (12 shorter events, 0.1 us)
Async XLA Ops:
  3.1 55.5 %copy-start.3 = (s32[64]{0:T(128)S(1)}, s32[64]{0:T(128)}, u32[]{:S(2)}) copy-start(s32[64]{0:T(128)} %param.3) | copy-start | bytes 772
  62.2 1.3 collective-permute-start
  63.5 3.9 %collective-permute-start.1 = (f32[64,64]{1,0:T(8,128)S(1)}, f32[64,64]{1,0:T(8,128)S(1)}, u32[]{:S(2)}, u32[]{:S(2)}) collective-permute-start(f32[64,64]{1,0:T(8,128)S(1)} %add.42), channel_id=1, source_target_pairs={{0,2},{1,3},{2,0},{3,1},{4,6},{5,7},{6,4},{7,5},{8,10},{9,11},{10,... | collective-permute-start | bytes 49160 | tf_op jit(solution)/shard_map/ppermute | solution.py:21
  67.4 5.1 %collective-permute-start.2 = (f32[64,64]{1,0:T(8,128)S(1)}, f32[64,64]{1,0:T(8,128)S(1)}, u32[]{:S(2)}, u32[]{:S(2)}) collective-permute-start(f32[64,64]{1,0:T(8,128)S(1)} %add.43), channel_id=1, source_target_pairs={{0,6},{1,7},{2,4},{3,5},{4,2},{5,3},{6,0},{7,1},{8,14},{9,15},{10,... | collective-permute-start | bytes 49160 | tf_op jit(solution)/shard_map/ppermute | solution.py:21
  72.5 3.9 %collective-permute-start.3 = (f32[64,64]{1,0:T(8,128)S(1)}, f32[64,64]{1,0:T(8,128)S(1)}, u32[]{:S(2)}, u32[]{:S(2)}) collective-permute-start(f32[64,64]{1,0:T(8,128)S(1)} %add.44), channel_id=1, source_target_pairs={{0,8},{8,0},{16,24},{24,16},{32,40},{40,32},{48,56},{56,48},{64,72... | collective-permute-start | bytes 49160 | tf_op jit(solution)/shard_map/ppermute | solution.py:21
  76.5 5.1 %collective-permute-start.4 = (f32[64,64]{1,0:T(8,128)S(1)}, f32[64,64]{1,0:T(8,128)S(1)}, u32[]{:S(2)}, u32[]{:S(2)}) collective-permute-start(f32[64,64]{1,0:T(8,128)S(1)} %add.45), channel_id=1, source_target_pairs={{0,24},{8,16},{16,8},{24,0},{32,56},{40,48},{48,40},{56,32},{64,88... | collective-permute-start | bytes 49160 | tf_op jit(solution)/shard_map/ppermute | solution.py:21
  81.6 3.9 %collective-permute-start.5 = (f32[64,64]{1,0:T(8,128)S(1)}, f32[64,64]{1,0:T(8,128)S(1)}, u32[]{:S(2)}, u32[]{:S(2)}) collective-permute-start(f32[64,64]{1,0:T(8,128)S(1)} %add.46), channel_id=1, source_target_pairs={{0,32},{8,40},{16,48},{24,56},{32,0},{40,8},{48,16},{56,24},{64,96... | collective-permute-start | bytes 49160 | tf_op jit(solution)/shard_map/ppermute | solution.py:21
  85.5 5.1 %collective-permute-start.6 = (f32[64,64]{1,0:T(8,128)S(1)}, f32[64,64]{1,0:T(8,128)S(1)}, u32[]{:S(2)}, u32[]{:S(2)}) collective-permute-start(f32[64,64]{1,0:T(8,128)S(1)} %add.47), channel_id=1, source_target_pairs={{0,96},{8,104},{16,112},{24,120},{32,64},{40,72},{48,80},{56,88},{... | collective-permute-start | bytes 49160 | tf_op jit(solution)/shard_map/ppermute | solution.py:21
  100.9 1.8 %copy-start = (f32[64,8192]{1,0:T(8,128)}, f32[64,8192]{1,0:T(8,128)S(1)}, u32[]{:S(2)}) copy-start(f32[64,8192]{1,0:T(8,128)S(1)} %fusion.7) | copy-start | bytes 6291460
  102.7 1.3 collective-permute-start.7
  104.0 3.9 %collective-permute-start.8 = (f32[64,64]{1,0:T(8,128)S(1)}, f32[64,64]{1,0:T(8,128)S(1)}, u32[]{:S(2)}, u32[]{:S(2)}) collective-permute-start(f32[64,64]{1,0:T(8,128)S(1)} %add.49), channel_id=1, source_target_pairs={{0,2},{1,3},{2,0},{3,1},{4,6},{5,7},{6,4},{7,5},{8,10},{9,11},{10,... | collective-permute-start | bytes 49160 | tf_op jit(solution)/shard_map/ppermute | solution.py:21
  108.0 5.1 %collective-permute-start.9 = (f32[64,64]{1,0:T(8,128)S(1)}, f32[64,64]{1,0:T(8,128)S(1)}, u32[]{:S(2)}, u32[]{:S(2)}) collective-permute-start(f32[64,64]{1,0:T(8,128)S(1)} %add.50), channel_id=1, source_target_pairs={{0,6},{1,7},{2,4},{3,5},{4,2},{5,3},{6,0},{7,1},{8,14},{9,15},{10,... | collective-permute-start | bytes 49160 | tf_op jit(solution)/shard_map/ppermute | solution.py:21
  113.1 3.9 %collective-permute-start.10 = (f32[64,64]{1,0:T(8,128)S(1)}, f32[64,64]{1,0:T(8,128)S(1)}, u32[]{:S(2)}, u32[]{:S(2)}) collective-permute-start(f32[64,64]{1,0:T(8,128)S(1)} %add.51), channel_id=1, source_target_pairs={{0,8},{8,0},{16,24},{24,16},{32,40},{40,32},{48,56},{56,48},{64,72... | collective-permute-start | bytes 49160 | tf_op jit(solution)/shard_map/ppermute | solution.py:21
  117.0 5.1 %collective-permute-start.11 = (f32[64,64]{1,0:T(8,128)S(1)}, f32[64,64]{1,0:T(8,128)S(1)}, u32[]{:S(2)}, u32[]{:S(2)}) collective-permute-start(f32[64,64]{1,0:T(8,128)S(1)} %add.52), channel_id=1, source_target_pairs={{0,24},{8,16},{16,8},{24,0},{32,56},{40,48},{48,40},{56,32},{64,88... | collective-permute-start | bytes 49160 | tf_op jit(solution)/shard_map/ppermute | solution.py:21
  122.1 3.9 %collective-permute-start.12 = (f32[64,64]{1,0:T(8,128)S(1)}, f32[64,64]{1,0:T(8,128)S(1)}, u32[]{:S(2)}, u32[]{:S(2)}) collective-permute-start(f32[64,64]{1,0:T(8,128)S(1)} %add.53), channel_id=1, source_target_pairs={{0,32},{8,40},{16,48},{24,56},{32,0},{40,8},{48,16},{56,24},{64,96... | collective-permute-start | bytes 49160 | tf_op jit(solution)/shard_map/ppermute | solution.py:21
  126.1 5.1 %collective-permute-start.13 = (f32[64,64]{1,0:T(8,128)S(1)}, f32[64,64]{1,0:T(8,128)S(1)}, u32[]{:S(2)}, u32[]{:S(2)}) collective-permute-start(f32[64,64]{1,0:T(8,128)S(1)} %add.54), channel_id=1, source_target_pairs={{0,96},{8,104},{16,112},{24,120},{32,64},{40,72},{48,80},{56,88},{... | collective-permute-start | bytes 49160 | tf_op jit(solution)/shard_map/ppermute | solution.py:21
  138.7 4.8 %copy-start.1 = (f32[64,64]{1,0:T(8,128)S(1)}, f32[64,64]{1,0:T(8,128)}, u32[]{:S(2)}) copy-start(f32[64,64]{1,0:T(8,128)} %get-tuple-element.9) | copy-start | bytes 49156
  138.7 4.8 %copy-start.2 = (f32[64,64]{1,0:T(8,128)S(1)}, f32[64,64]{1,0:T(8,128)}, u32[]{:S(2)}) copy-start(f32[64,64]{1,0:T(8,128)} %get-tuple-element.8) | copy-start | bytes 49156
where the time goes:
time: 145 us; the launch traced here: 144 us
  blocking collectives  55.5 us (38%)
  waiting for transfers between devices  38.6 us (27%)
  starting transfers between devices  18.2 us (13%)
  Pallas kernels  13.9 us (10%)
  matrix products  13.6 us (9%)
  local copies, waits for them, and re-layouts  2.5 us (2%)
    all_to_all x1, blocking collectives, per_device(): lax.all_to_all(stored, 'store', split_axis=1, concat_axis=0, tiled=True)  55.5 us
    ppermute x14, waiting for transfers between devices, neighbour_sum(): value = value + lax.ppermute(value, axis, pairs)  38.6 us
    ppermute x14, starting transfers between devices, neighbour_sum(): value = value + lax.ppermute(value, axis, pairs)  18.2 us
    pallas_call x2, Pallas kernels, factor_of(): return pl.pallas_call(factor_kernel, out_shape=(shape, shape))(gram)  13.9 us
    dot_general x6, matrix products, dot(): return jnp.dot(a, b, precision=HIGHEST, preferred_element_type=jnp.float32)  13.6 us
  transfers between devices with their start and end apart: 14, of which 14 were waited for; matrix products, arithmetic and copies ran while one was open for 0% of the time, Pallas kernels for 0%

commit v1 on v0

v1 whole, which is shorter than its diff:
```python
import math

import jax
import jax.numpy as jnp
from jax import lax
from jax.experimental import pallas as pl
from jax.experimental.pallas import tpu as pltpu
from jax.sharding import PartitionSpec as P

HIGHEST = lax.Precision.HIGHEST
UP = 2.0**24


def dot(a, b):
    return jnp.dot(a, b, precision=HIGHEST, preferred_element_type=jnp.float32)


def iota(shape, dim):
    return lax.broadcasted_iota(jnp.int32, shape, dim)


def power_above(value):
    c, inverse = jnp.ones_like(value), jnp.ones_like(value)
    for e in (64, 32, 16, 8, 4, 2, 1):
        big = value * inverse > 2.0**e * 0.5
        c = jnp.where(big, c * 2.0**e, c)
        inverse = jnp.where(big, inverse * 2.0**-e, inverse)
    for e in (64, 32, 16, 8, 4, 2, 1):
        small = (value * inverse <= 2.0**-e) & (c > 2.0 ** (e - 126))
        c = jnp.where(small, c * 2.0**-e, c)
        inverse = jnp.where(small, inverse * 2.0**e, inverse)
    return c, inverse


def row_of(column):
    n = column.shape[0]
    return jnp.sum(jnp.where(iota((n, n), 0) == iota((n, n), 1), column, 0.0), axis=0, keepdims=True)


def two_sum(a, b):
    s = a + b
    t = s - a
    return s, (a - (s - t)) + (b - t)


def pair_add(first, second):
    s, e = two_sum(first[0], second[0])
    return s, (first[1] + second[1]) + e * UP


def nearest(x):
    return lax.round(x, lax.RoundingMethod.TO_NEAREST_EVEN)


def pieces(x, count):
    out = []
    t = x * 256.0
    for i in range(count):
        n = nearest(t)
        out.append(n)
        t = (t - n) * 512.0
    return out, t


def levels_to_pair(levels):
    hi, lo = levels[0], jnp.zeros_like(levels[0])
    for l in range(1, len(levels)):
        hi, e = two_sum(hi, levels[l] * 2.0 ** (-9 * l))
        lo = lo + e
    return two_sum(hi, lo)


def eliminate(gram, block=8):
    n = gram.shape[0]
    rows, columns = iota((n, n), 0), iota((n, n), 1)
    whole = jnp.concatenate([gram, (rows == columns).astype(jnp.float32)], axis=1)
    lane = iota((8, 2 * n), 1)
    sub = iota((8, 2 * n), 0)
    g = n // 8
    blocks = [whole[8 * i : 8 * i + 8] for i in range(g)]
    done = []
    for b in range(g):
        cols = {}
        for i in range(b, g):
            for q in range(8):
                j = 8 * b + q
                cols[i, q] = jnp.broadcast_to(blocks[i][:, j : j + 1], (8, 2 * n))
        mult = {}
        pivots = jnp.ones((8, 2 * n), jnp.float32)
        rowsb = blocks[b]
        for q in range(8):
            pivot = jnp.broadcast_to(cols[b, q][q : q + 1], (8, 2 * n))
            pivots = jnp.where(sub == q, pivot, pivots)
            w = 1.0 / pivot
            row = jnp.broadcast_to(rowsb[q : q + 1], (8, 2 * n))
            for i in range(b, g):
                m = cols[i, q] * w
                if i == b:
                    m = jnp.where(sub > q, m, 0.0)
                mult[i, q] = m
            rowsb = rowsb - mult[b, q] * row
            for r in range(q + 1, 8):
                a = jnp.broadcast_to(cols[b, r][q : q + 1], (8, 2 * n))
                for i in range(b, g):
                    cols[i, r] = cols[i, r] - mult[i, q] * a
        for i in range(b + 1, g):
            value = blocks[i]
            for q in range(8):
                value = value - mult[i, q] * jnp.broadcast_to(rowsb[q : q + 1], (8, 2 * n))
            blocks[i] = value
        s = lax.rsqrt(pivots)
        s = s * (1.5 - 0.5 * pivots * s * s)
        done.append(rowsb * s)
    whole = jnp.concatenate(done, axis=0)
    upper = jnp.where(rows <= columns, whole[:, :n], 0.0)
    lower = jnp.where(rows >= columns, whole[:, n:], 0.0)
    return upper, lower


def bf16_dot(a, b):
    return lax.dot_general(a, b, (((1,), (0,)), ((), ())), preferred_element_type=jnp.float32)


def wide_product(left, right, keep):
    n = left[0].shape[0]
    na, nb = len(left), len(right)
    l = jnp.concatenate([x.astype(jnp.bfloat16) for x in left], axis=0)
    r = jnp.concatenate([x.astype(jnp.bfloat16) for x in right], axis=1)
    m = bf16_dot(l, r)
    out = []
    for lev in range(keep):
        acc = None
        for a in range(na):
            c = lev - a
            if 0 <= c < nb:
                t = m[a * n : (a + 1) * n, c * n : (c + 1) * n]
                acc = t if acc is None else acc + t
        out.append(acc)
    return out


def second_gram(hi, lo, lower):
    first, rest = pieces(hi, 3)
    rest = rest + lo * (2.0 ** (8 + 27) / UP)
    out = []
    for _ in range(3):
        n = nearest(rest)
        out.append(n)
        rest = (rest - n) * 512.0
    g = first + out
    top = jnp.max(jnp.abs(lower), axis=1, keepdims=True)
    u, v = power_above(top)
    ls, _ = pieces(lower * v, 4)
    lt = [x.T for x in ls]
    ur = row_of(u)
    lev = wide_product(g, lt, 7)
    ch, cl = levels_to_pair(lev)
    scale = ur * 2.0**-16
    ch, cl = ch * scale, cl * scale
    cs, rest = pieces(ch * 0.5, 3)
    rest = rest + cl * (0.5 * 2.0 ** (8 + 27))
    for _ in range(2):
        n = nearest(rest)
        cs.append(n)
        rest = (rest - n) * 512.0
    lev = wide_product(ls, cs, 7)
    h, l = levels_to_pair(lev)
    return (h + l) * (u * 2.0**-15)


def finish(hi, lo, count):
    n = hi.shape[0]
    eye = iota((n, n), 0) == iota((n, n), 1)
    diag = jnp.sum(jnp.where(eye, hi, 0.0), axis=1, keepdims=True)
    d, di = power_above(jnp.sqrt(diag))
    dr, dir_ = row_of(d), row_of(di)
    hs = (hi * di) * dir_
    ls = (lo * di) * dir_
    r1, l1 = eliminate(hs)
    g2 = second_gram(hs, ls, l1)
    r2, l2 = eliminate(g2)
    scale = math.sqrt(count)
    w = dot(l2, l1) * (dir_ * scale)
    factor = dot(r2, r1) * (dr * (1.0 / scale))
    return w, factor, g2


def combine(acc, c):
    n = acc.shape[0] // 4
    cr = row_of(c)
    levels = []
    for lev in range(7):
        t = None
        for a in range(4):
            b = lev - a
            if 0 <= b < 4:
                x = acc[a * n : (a + 1) * n, b * n : (b + 1) * n]
                t = x if t is None else t + x
        levels.append(t)
    hi = jnp.zeros((n, n), jnp.float32)
    lo = jnp.zeros((n, n), jnp.float32)
    for lev, t in enumerate(levels):
        high = lax.shift_right_arithmetic(t, 14)
        low = (t - lax.shift_left(high, 14)).astype(jnp.float32) * 2.0 ** (-9 * lev)
        high = high.astype(jnp.float32) * 2.0 ** (14 - 9 * lev)
        hi, e = two_sum(hi, high)
        lo = lo + e
        hi, e = two_sum(hi, low)
        lo = lo + e
    hi, lo = two_sum(hi, lo)
    f = 2.0**-16
    return ((hi * f) * c) * cr, (((lo * (f * UP)) * c) * cr)


STEP = 256


def gram_kernel(panel_ref, out_ref, sum_ref):
    n, columns = panel_ref.shape
    c, inverse = power_above(jnp.max(jnp.abs(panel_ref[...]), axis=1, keepdims=True))
    sum_ref[...] = jnp.zeros_like(sum_ref)

    def step(k, carry):
        block = panel_ref[:, pl.ds(pl.multiple_of(k * STEP, STEP), STEP)]
        parts, _ = pieces(block * inverse, 4)
        x = jnp.concatenate([p.astype(jnp.bfloat16) for p in parts], axis=0)
        h = lax.dot_general(x, x, (((1,), (1,)), ((), ())), preferred_element_type=jnp.float32)
        sum_ref[...] += h.astype(jnp.int32)
        return carry

    lax.fori_loop(0, columns // STEP, step, 0, unroll=4)
    hi, lo = combine(sum_ref[...], c)
    pair = jnp.concatenate([hi, lo], axis=1)
    for i in range(out_ref.shape[0]):
        out_ref[i] = pair


def pair_sum(ref):
    lane = iota(ref.shape[1:], 1)
    half = ref.shape[2] // 2
    total, rest = ref[0], jnp.zeros(ref.shape[1:], jnp.float32)
    for i in range(1, ref.shape[0]):
        total, e = two_sum(total, ref[i])
        rest = rest + e
    rest = jnp.where(lane < half, rest * UP, 0.0)
    return total + pltpu.roll(rest, half, 1)


def sum_kernel(in_ref, out_ref):
    total = pair_sum(in_ref)
    for i in range(out_ref.shape[0]):
        out_ref[i] = total


def finish_kernel(count, in_ref, w_ref, factor_ref):
    total = pair_sum(in_ref)
    n = total.shape[0]
    w, factor, _ = finish(total[:, :n], total[:, n:], count)
    w_ref[...] = w
    factor_ref[...] = factor


def per_device(stored, snap_slot):
    received = lax.all_to_all(stored, "store", split_axis=1, concat_axis=0, tiled=True)
    places = jnp.arange(received.shape[0], dtype=jnp.int32)
    selector = (snap_slot[:, None] == places[None, :]).astype(jnp.float32)
    panel = dot(selector, received)
    n, columns = panel.shape
    store, rows = lax.axis_size("store"), lax.axis_size("rows")
    f32 = jnp.float32
    pairs = pl.pallas_call(
        gram_kernel,
        out_shape=jax.ShapeDtypeStruct((store, n, 2 * n), f32),
        scratch_shapes=[pltpu.VMEM((4 * n, 4 * n), jnp.int32)],
        compiler_params=pltpu.CompilerParams(vmem_limit_bytes=32 * 2**20),
    )(panel)
    pairs = lax.all_to_all(pairs, "store", split_axis=0, concat_axis=0, tiled=True)
    pairs = pl.pallas_call(sum_kernel, out_shape=jax.ShapeDtypeStruct((rows, n, 2 * n), f32))(pairs)
    pairs = lax.all_to_all(pairs, "rows", split_axis=0, concat_axis=0, tiled=True)
    square = jax.ShapeDtypeStruct((n, n), f32)
    weights, factor = pl.pallas_call(
        lambda *refs: finish_kernel(columns * store * rows, *refs), out_shape=(square, square)
    )(pairs)
    return (dot(weights, panel), factor)


def solution(mesh):
    in_specs = (P("store", "rows"), P())
    out_specs = (P(None, ("rows", "store")), P())
    return jax.shard_map(
        per_device, mesh=mesh, in_specs=in_specs, out_specs=out_specs, check_vma=False
    )
```

time: 145 us -> 107 us (0.74)
  waiting for transfers between devices: 38.6 us -> 0 us
  blocking collectives: 55.5 us -> 84.4 us
  starting transfers between devices: 18.2 us -> 0 us
  matrix products: 13.6 us -> 5.75 us
    ppermute x14 -> x0, waiting for transfers between devices: 38.6 us -> none  [neighbour_sum(): value = value + lax.ppermute(value, axis, pairs)]
    all_to_all x0 -> x2, blocking collectives: none -> 28.9 us  [the longest x1 18.3 us: per_device(): lax.all_to_all(pairs, 'rows', split_axis=0, concat_axis=0, tiled=True)]
    ppermute x14 -> x0, starting transfers between devices: 18.2 us -> none  [neighbour_sum(): value = value + lax.ppermute(value, axis, pairs)]
    dot_general x6 -> x2, matrix products: 13.6 us -> 5.75 us  [dot(): return jnp.dot(a, b, precision=HIGHEST, preferred_element_type=jnp.float32)]
    pallas_call x2 -> x3, Pallas kernels: 13.9 us -> 13 us  [the longest x1 7.45 us: per_device(): pl.pallas_call(lambda *refs: finish_kernel(columns * store * rows, *refs)...]
  transfers between devices with their start and end apart: 14 -> 0, of which waited for: 14 -> 0; matrix products, arithmetic and copies ran while one was open for 0% -> 0% of each run, Pallas kernels for 0% -> 0%
where the time goes in v1:
time: 107 us; the launch traced here: 106 us
  blocking collectives  84.4 us (79%)
  Pallas kernels  13 us (12%)
  matrix products  5.75 us (5%)
  local copies, waits for them, and re-layouts  2.49 us (2%)
    all_to_all x1, blocking collectives, per_device(): lax.all_to_all(stored, 'store', split_axis=1, concat_axis=0, tiled=True)  55.5 us
    all_to_all x1, blocking collectives, per_device(): lax.all_to_all(pairs, 'rows', split_axis=0, concat_axis=0, tiled=True)  18.3 us
    all_to_all x1, blocking collectives, per_device(): lax.all_to_all(pairs, 'store', split_axis=0, concat_axis=0, tiled=True)  10.6 us
    pallas_call x1, Pallas kernels, per_device(): pl.pallas_call(lambda *refs: finish_kernel(columns * store * rows, *refs)...  7.45 us
    dot_general x2, matrix products, dot(): return jnp.dot(a, b, precision=HIGHEST, preferred_element_type=jnp.float32)  5.75 us
    pallas_call x1, Pallas kernels, per_device(): pl.pallas_call(gram_kernel, out_shape=jax.ShapeDtypeStruct((store, n, 2 *...  3.67 us
    all_to_all x1, local copies, waits for them, and re-layouts, per_device(): lax.all_to_all(stored, 'store', split_axis=1, concat_axis=0, tiled=True)  2.49 us

profile of v1, /device:TPU:0, one launch (start us, length us, event | category | flops | bytes accessed | tf_op | source)
XLA Modules:
  0.0 106.3 jit_solution(11188995417416301111)
XLA Ops:
  0.6 2.5 %copy.8 = f32[2,8,8,8192]{3,2,0,1:T(8,128)S(1)} copy(f32[2,8,8,8192]{3,2,1,0:T(8,128)} %bitcast.12) | data formatting | bytes 8388608 | tf_op jit(solution)/shard_map/all_to_all | solution.py:264
  3.1 0.0 copy-start
  3.1 55.5 %all_to_all.29 = f32[16,8,8192]{2,0,1:T(8,128)S(1)} all-to-all(f32[16,8,8192]{2,0,1:T(8,128)S(1)} %bitcast.11), channel_id=1, replica_groups=mesh['rows'=16,'store'=8] {'store'}, dimensions={1} | all-to-all | bytes 8388608 | tf_op jit(solution)/shard_map/all_to_all | solution.py:264
  58.7 0.0 copy-done
  58.7 1.7 %fusion.panel_ref = f32[64,8192]{1,0:T(8,128)S(1)} fusion(f32[128,8192]{1,0:T(8,128)S(1)} %bitcast.10, s32[64]{0:T(128)S(1)} %copy-done), kind=kOutput, calls=%fused_computation.2 | convolution fusion | flops 805314560 | bytes 6291712 | tf_op jit(solution)/shard_map/dot_general | solution.py:15
  60.4 3.7 %shard_map.41 = f32[8,64,128]{2,1,0:T(8,128)S(1)} custom-call(f32[64,8192]{1,0:T(8,128)S(1)} %fusion.panel_ref), custom_call_target="tpu_custom_call" | custom-call | tf_op jit(solution)/shard_map/pallas_call | solution.py:271
  64.1 10.6 %all_to_all.30.in_ref = f32[8,64,128]{2,1,0:T(8,128)} all-to-all(f32[8,64,128]{2,1,0:T(8,128)S(1)} %shard_map.41), channel_id=1, replica_groups=mesh['rows'=16,'store'=8] {'store'}, dimensions={0} | all-to-all | bytes 524288 | tf_op jit(solution)/shard_map/all_to_all | solution.py:277
  74.7 1.9 %shard_map.42 = f32[16,64,128]{2,1,0:T(8,128)} custom-call(f32[8,64,128]{2,1,0:T(8,128)} %all_to_all.30.in_ref), custom_call_target="tpu_custom_call" | custom-call | tf_op jit(solution)/shard_map/pallas_call | solution.py:278
  76.6 18.3 %all_to_all.31.refs_0_ = f32[16,64,128]{2,1,0:T(8,128)} all-to-all(f32[16,64,128]{2,1,0:T(8,128)} %shard_map.42), channel_id=1, replica_groups=mesh['rows'=16,'store'=8] {'rows'}, dimensions={0} | all-to-all | bytes 1048576 | tf_op jit(solution)/shard_map/all_to_all | solution.py:279
  94.8 7.4 %shard_map.43 = (f32[64,64]{1,0:T(8,128)}, f32[64,64]{1,0:T(8,128)}) custom-call(f32[16,64,128]{2,1,0:T(8,128)} %all_to_all.31.refs_0_), custom_call_target="tpu_custom_call" | custom-call | tf_op jit(solution)/shard_map/pallas_call | solution.py:281
  102.3 4.0 %fusion.2 = f32[64,8192]{1,0:T(8,128)} fusion(f32[64,64]{1,0:T(8,128)} %get-tuple-element.4, f32[64,8192]{1,0:T(8,128)S(1)} %fusion.panel_ref), kind=kOutput, calls=%fused_computation.4 | convolution fusion | flops 402653184 | bytes 4210688 | tf_op jit(solution)/shard_map/dot_general | solution.py:15
Async XLA Ops:
  3.1 55.5 %copy-start = (s32[64]{0:T(128)S(1)}, s32[64]{0:T(128)}, u32[]{:S(2)}) copy-start(s32[64]{0:T(128)} %param.3) | copy-start | bytes 772

commit v2 on v1

--- a/solution.py
+++ b/solution.py
@@ -213,11 +213,71 @@
 
 
 STEP = 256
-
-
-def gram_kernel(panel_ref, out_ref, sum_ref):
+CORES = 2
+BIG = pltpu.CompilerParams(vmem_limit_bytes=32 * 2**20)
+
+
+def thirds(x):
+    high = x.astype(jnp.bfloat16)
+    rest = x - high.astype(jnp.float32)
+    mid = rest.astype(jnp.bfloat16)
+    low = (rest - mid.astype(jnp.float32)).astype(jnp.bfloat16)
+    return jnp.concatenate([high, mid, low], axis=0)
+
+
+def place():
+    store = lax.axis_index("store")
+    return store // CORES, store % CORES
+
+
+def part_kernel(distances, chips, stored_ref, *refs):
+    outs, sems = refs[-1 - len(distances) : -1], refs[-1]
+    width = outs[0].shape[1]
+    z, core = place()
+    copies = []
+    for d, out in zip(distances, outs):
+        owner = lax.rem(z + d, chips) * CORES + 1 - core
+        start = pl.multiple_of(owner * width, width)
+        copies.append(pltpu.make_async_copy(stored_ref.at[:, pl.ds(start, width)], out, sems.at[len(copies)]))
+    for copy in copies:
+        copy.start()
+    for copy in copies:
+        copy.wait()
+
+
+def pick_kernel(distance, chips, stored_ref, other_ref, selector_ref, out_ref, own_ref, sem):
+    width = out_ref.shape[1]
+    z, core = place()
+    owner = lax.rem(z + distance, chips) * CORES + core
+    start = pl.multiple_of(owner * width, width)
+    copy = pltpu.make_async_copy(stored_ref.at[:, pl.ds(start, width)], own_ref, sem)
+    copy.start()
+    selector = selector_ref[...]
+    copy.wait()
+
+    def step(k, carry):
+        block = pl.ds(pl.multiple_of(k * STEP, STEP), STEP)
+        both = jnp.concatenate([own_ref[:, block], other_ref[:, block]], axis=0)
+        out_ref[:, block] = bf16_dot(selector, thirds(both))
+        return carry
+
+    lax.fori_loop(0, width // STEP, step, 0, unroll=8)
+
+
+def gram_kernel(*refs):
+    blocks_refs, (selector_ref, panel_ref, out_ref, sum_ref) = refs[:-4], refs[-4:]
     n, columns = panel_ref.shape
-    c, inverse = power_above(jnp.max(jnp.abs(panel_ref[...]), axis=1, keepdims=True))
+    selector = selector_ref[...]
+
+    def gather(k, top):
+        block = pl.ds(pl.multiple_of(k * STEP, STEP), STEP)
+        got = jnp.concatenate([ref[:, block] for ref in blocks_refs], axis=0)
+        rows = bf16_dot(selector, thirds(got))
+        panel_ref[:, block] = rows
+        return jnp.maximum(top, jnp.abs(rows))
+
+    top = lax.fori_loop(0, columns // STEP, gather, jnp.zeros((n, STEP), jnp.float32), unroll=8)
+    c, inverse = power_above(jnp.max(top, axis=1, keepdims=True))
     sum_ref[...] = jnp.zeros_like(sum_ref)
 
     def step(k, carry):
@@ -229,10 +289,37 @@
         return carry
 
     lax.fori_loop(0, columns // STEP, step, 0, unroll=4)
-    hi, lo = combine(sum_ref[...], c)
-    pair = jnp.concatenate([hi, lo], axis=1)
+    packed = pack(*combine(sum_ref[...], c))
     for i in range(out_ref.shape[0]):
-        out_ref[i] = pair
+        out_ref[i] = packed
+
+
+def pack(hi, lo):
+    h = hi.shape[0] // 2
+    rows, columns = iota((h, h), 0), iota((h, h), 1)
+    wide, diagonals = [], []
+    for x in (hi, lo):
+        a, b, c = x[:h, :h], x[:h, h:], x[h:, h:]
+        diagonal = jnp.sum(jnp.where(rows == columns, c, 0.0), axis=0, keepdims=True)
+        wide += [jnp.where(columns >= rows, a, c), b]
+        diagonals += [diagonal, jnp.zeros_like(diagonal)]
+    tail = jnp.broadcast_to(jnp.concatenate(diagonals, axis=1), (8, 4 * h))
+    return jnp.concatenate([jnp.concatenate(wide, axis=1), tail], axis=0)
+
+
+def unpack(packed):
+    h = packed.shape[1] // 4
+    rows, columns = iota((h, h), 0), iota((h, h), 1)
+    main = packed[:h]
+    turned = main.T
+    out = []
+    for i in (0, 2 * h):
+        m, mt = main[:, i : i + h], turned[i : i + h]
+        b, bt = main[:, i + h : i + 2 * h], turned[i + h : i + 2 * h]
+        a = jnp.where(columns >= rows, m, mt)
+        c = jnp.where(columns < rows, m, jnp.where(columns > rows, mt, packed[h : h + 1, i : i + h]))
+        out.append(jnp.concatenate([jnp.concatenate([a, b], axis=1), jnp.concatenate([bt, c], axis=1)], axis=0))
+    return out
 
 
 def pair_sum(ref):
@@ -253,35 +340,129 @@
 
 
 def finish_kernel(count, in_ref, w_ref, factor_ref):
-    total = pair_sum(in_ref)
-    n = total.shape[0]
-    w, factor, _ = finish(total[:, :n], total[:, n:], count)
+    w, factor, _ = finish(*unpack(pair_sum(in_ref)), count)
     w_ref[...] = w
     factor_ref[...] = factor
 
 
+def float_array(*shape):
+    return jax.ShapeDtypeStruct(shape, jnp.float32)
+
+
+def modes_kernel(weights_ref, panel_ref, out_ref):
+    n = weights_ref.shape[0]
+    w = thirds(weights_ref[...])
+    first, second, third = w[:n], w[n : 2 * n], w[2 * n :]
+    none = jnp.zeros_like(first)
+    left = jnp.concatenate(
+        [
+            jnp.concatenate([first, first, first], axis=1),
+            jnp.concatenate([second, second, none], axis=1),
+            jnp.concatenate([third, none, none], axis=1),
+        ],
+        axis=0,
+    )
+
+    def step(k, carry):
+        block = pl.ds(pl.multiple_of(k * STEP, STEP), STEP)
+        got = bf16_dot(left, thirds(panel_ref[:, block]))
+        out_ref[:, block] = (got[2 * n :] + got[n : 2 * n]) + got[:n]
+        return carry
+
+    lax.fori_loop(0, out_ref.shape[1] // STEP, step, 0, unroll=True)
+
+
+def swapped(distances, chips, stored, *after):
+    store = lax.axis_size("store")
+    parts = pl.pallas_call(
+        lambda *refs: part_kernel(distances, chips, *refs),
+        out_shape=(float_array(stored.shape[0], stored.shape[1] // store),) * len(distances),
+        in_specs=[pl.BlockSpec(memory_space=pl.ANY)] * (1 + len(after)),
+        scratch_shapes=[pltpu.SemaphoreType.DMA((len(distances),))],
+        compiler_params=BIG,
+    )(stored, *after)
+    swap = [(i, i ^ 1) for i in range(store)]
+    return [lax.ppermute(part, "store", swap) for part in parts]
+
+
+def picked(distance, chips, stored, other, pick):
+    slots, width = other.shape
+    return pl.pallas_call(
+        lambda *refs: pick_kernel(distance, chips, *refs),
+        out_shape=float_array(pick.shape[0], width),
+        in_specs=[pl.BlockSpec(memory_space=pl.ANY)] + [pl.BlockSpec(memory_space=pltpu.VMEM)] * 2,
+        scratch_shapes=[pltpu.VMEM((slots, width), jnp.float32), pltpu.SemaphoreType.DMA(())],
+        compiler_params=BIG,
+    )(stored, other, pick)
+
+
+def relayout(capacity, stored, other, pick, chip, position):
+    n = chip.shape[0]
+    slots, width = other.shape
+    store = lax.axis_size("store")
+    chips = store // CORES
+    z, core = place()
+    pick = pick[:capacity]
+
+    def send(block, d):
+        return lax.ppermute(block, "store", [(i, (i + d * CORES) % store) for i in range(store)])
+
+    blocks = [None] * chips
+    block = picked(2, chips, stored, other, pick)
+    blocks[2] = send(block, 2)
+    rest = (1, 3, 0)
+    for d, other in zip(rest, swapped(rest, chips, stored, block)):
+        block = picked(d, chips, stored, other, pick)
+        blocks[d] = send(block, d) if d else block
+    source = lax.rem(z - chip + chips, chips) * capacity + position
+    gather = source[:, None] == jnp.arange(chips * capacity)[None, :]
+    gather = jnp.tile(gather.astype(jnp.bfloat16), (1, 3))
+    return pl.pallas_call(
+        gram_kernel,
+        out_shape=(float_array(n, width), float_array(store, n // 2 + 8, 2 * n)),
+        scratch_shapes=[pltpu.VMEM((4 * n, 4 * n), jnp.int32)],
+        compiler_params=BIG,
+    )(*blocks, gather)
+
+
 def per_device(stored, snap_slot):
-    received = lax.all_to_all(stored, "store", split_axis=1, concat_axis=0, tiled=True)
-    places = jnp.arange(received.shape[0], dtype=jnp.int32)
-    selector = (snap_slot[:, None] == places[None, :]).astype(jnp.float32)
-    panel = dot(selector, received)
-    n, columns = panel.shape
+    n = snap_slot.shape[0]
+    slots = stored.shape[0]
     store, rows = lax.axis_size("store"), lax.axis_size("rows")
-    f32 = jnp.float32
-    pairs = pl.pallas_call(
-        gram_kernel,
-        out_shape=jax.ShapeDtypeStruct((store, n, 2 * n), f32),
-        scratch_shapes=[pltpu.VMEM((4 * n, 4 * n), jnp.int32)],
-        compiler_params=pltpu.CompilerParams(vmem_limit_bytes=32 * 2**20),
-    )(panel)
+    columns, chips = stored.shape[1] // store, store // CORES
+    (other,) = swapped((2,), chips, stored)
+    z, core = place()
+    chip = snap_slot // (slots * CORES)
+    same = chip[:, None] == chip[None, :]
+    position = jnp.sum((same & (snap_slot[None, :] < snap_slot[:, None])).astype(jnp.int32), axis=1)
+    most = jnp.max(position) + 1
+    capacities = (16, 24, 32)
+    choice = sum((most > c).astype(jnp.int32) for c in capacities[:-1])
+    local = snap_slot - (chip * CORES + core) * slots
+    local = jnp.where(local < 0, local + 2 * slots, local)
+    order = jnp.arange(2 * slots)
+    chosen = (chip == z)[None, :] & (position[None, :] == order[:, None])
+    pick = jnp.any(chosen[:, None, :] & (local[None, None, :] == order[None, :, None]), axis=2)
+    pick = jnp.tile(pick.astype(jnp.bfloat16), (1, 3))
+    branches = [lambda *args, c=c: relayout(c, *args) for c in capacities]
+    panel, pairs = lax.switch(choice, branches, stored, other, pick, chip, position)
     pairs = lax.all_to_all(pairs, "store", split_axis=0, concat_axis=0, tiled=True)
-    pairs = pl.pallas_call(sum_kernel, out_shape=jax.ShapeDtypeStruct((rows, n, 2 * n), f32))(pairs)
+    pairs = pl.pallas_call(sum_kernel, out_shape=float_array(rows, n // 2 + 8, 2 * n))(pairs)
     pairs = lax.all_to_all(pairs, "rows", split_axis=0, concat_axis=0, tiled=True)
-    square = jax.ShapeDtypeStruct((n, n), f32)
     weights, factor = pl.pallas_call(
-        lambda *refs: finish_kernel(columns * store * rows, *refs), out_shape=(square, square)
+        lambda *refs: finish_kernel(columns * store * rows, *refs),
+        out_shape=(float_array(n, n),) * 2,
     )(pairs)
-    return (dot(weights, panel), factor)
+    wide = columns // 4
+    modes = pl.pallas_call(
+        modes_kernel,
+        grid=(columns // wide,),
+        out_shape=float_array(n, columns),
+        in_specs=[pl.BlockSpec((n, n), lambda i: (0, 0)), pl.BlockSpec((n, wide), lambda i: (0, i))],
+        out_specs=pl.BlockSpec((n, wide), lambda i: (0, i)),
+        compiler_params=BIG,
+    )(weights, panel)
+    return (modes, factor)
 
 
 def solution(mesh):

time: 107 us -> 96.8 us (0.905)
  blocking collectives: 84.4 us -> 26.4 us
  waiting for transfers between devices: 0 us -> 27.1 us
  Pallas kernels: 13 us -> 31.1 us
  starting transfers between devices: 0 us -> 6.85 us
  matrix products: 5.75 us -> 0 us
  other arithmetic: 0 us -> 1.58 us
    all_to_all x1 -> x0, blocking collectives: 55.5 us -> none  [per_device(): lax.all_to_all(stored, 'store', split_axis=1, concat_axis=0, tiled=True)]
    ppermute x0 -> x7, waiting for transfers between devices: none -> 27.1 us  [the longest x3 25.1 us: send(): lax.ppermute(block, 'store', [(i, (i + d * CORES) % store) for i in range...]
    pallas_call x2 -> x9, Pallas kernels: 5.56 us -> 23.6 us  [the longest x4 9.5 us: picked(): pl.pallas_call(lambda *refs: pick_kernel(distance, chips, *refs), out_sha...]
    ppermute x0 -> x7, starting transfers between devices: none -> 6.85 us  [the longest x3 6.12 us: send(): lax.ppermute(block, 'store', [(i, (i + d * CORES) % store) for i in range...]
    dot_general x2 -> x0, matrix products: 5.75 us -> none  [dot(): return jnp.dot(a, b, precision=HIGHEST, preferred_element_type=jnp.float32)]
    all_to_all x1 -> x0, local copies, waits for them, and re-layouts: 2.49 us -> none  [per_device(): lax.all_to_all(stored, 'store', split_axis=1, concat_axis=0, tiled=True)]
    all_to_all x1, blocking collectives: 18.3 us -> 16.1 us  [per_device(): lax.all_to_all(pairs, 'rows', split_axis=0, concat_axis=0, tiled=True)]
  transfers between devices with their start and end apart: 0 -> 7, of which waited for: 0 -> 3; matrix products, arithmetic and copies ran while one was open for 0% -> 2% of each run, Pallas kernels for 0% -> 7%
where the time goes in v2:
time: 96.8 us; the launch traced here: 96.2 us
  Pallas kernels  31.1 us (32%)
  waiting for transfers between devices  27.1 us (28%)
  blocking collectives  26.4 us (27%)
  starting transfers between devices  6.85 us (7%)
  local copies, waits for them, and re-layouts  1.77 us (2%)
  other arithmetic  1.58 us (2%)
  between operations  1.38 us (1%)
    ppermute x3, waiting for transfers between devices, send(): lax.ppermute(block, 'store', [(i, (i + d * CORES) % store) for i in range...  25.1 us
    all_to_all x1, blocking collectives, per_device(): lax.all_to_all(pairs, 'rows', split_axis=0, concat_axis=0, tiled=True)  16.1 us
    all_to_all x1, blocking collectives, per_device(): lax.all_to_all(pairs, 'store', split_axis=0, concat_axis=0, tiled=True)  10.3 us
    pallas_call x4, Pallas kernels, picked(): pl.pallas_call(lambda *refs: pick_kernel(distance, chips, *refs), out_sha...  9.5 us
    pallas_call x1, Pallas kernels, per_device(): pl.pallas_call(lambda *refs: finish_kernel(columns * store * rows, *refs)...  7.51 us
    ppermute x3, starting transfers between devices, send(): lax.ppermute(block, 'store', [(i, (i + d * CORES) % store) for i in range...  6.12 us
    pallas_call x1, Pallas kernels, relayout(): pl.pallas_call(gram_kernel, out_shape=(float_array(n, width), float_array...  5.73 us
    pallas_call x1, Pallas kernels, per_device(): pl.pallas_call(modes_kernel, grid=(columns // wide,), out_shape=float_arr...  4.51 us
  transfers between devices with their start and end apart: 7, of which 3 were waited for; matrix products, arithmetic and copies ran while one was open for 2% of the time, Pallas kernels for 7%

profile of v2, /device:TPU:0, one launch (start us, length us, event | category | flops | bytes accessed | tf_op | source)
XLA Modules:
  0.0 96.2 jit_solution(2274526282410366255)
XLA Ops:
  0.6 0.0 copy-start.6
  0.6 1.1 %shard_map.41 = f32[16,8192]{1,0:T(8,128)S(1)} custom-call(f32[16,65536]{1,0:T(8,128)} %refs_0_.1), custom_call_target="tpu_custom_call" | custom-call | tf_op jit(solution)/shard_map/pallas_call | solution.py:377
  1.7 0.1 collective-permute-start.18
  1.8 0.0 copy-done.6
  1.9 0.2 convert_reduce_fusion
  2.0 0.6 reduce_max.9
  3.4 0.6 and_reduce_fusion
  4.0 0.1 tile.27
  4.1 0.0 collective-permute-done.18
  4.1 51.2 %conditional.1 = ((f32[64,8192]{1,0:T(8,128)}, f32[8,40,128]{2,1,0:T(8,128)S(1)})) conditional(s32[]{:T(128)} %clamp.3, (bf16[32,96]{1,0:T(8,128)(2,1)S(1)}, f32[16,65536]{1,0:T(8,128)}, f32[16,8192]{1,0:T(8,128)S(1)}, s32[64]{0:T(128)S(1)}, s32[64]{0:T(128)S(1)}) %tuple.17, (bf16[32,96]{1,0:T(8,128)(2,1)S(1)}, ...), branch_computations={%region_3.4_spmd, %region_4.5_spmd, %region_5.6_spmd} | conditional | flops 17041 | bytes 37930456 | solution.py:448
  4.2 0.0 copy-start.4
  4.2 0.8 copy-done.4
  5.0 0.0 copy-start.2
  5.0 3.2 %branch_1_fun.6.refs_1_ = f32[24,8192]{1,0:T(8,128)S(1)} custom-call(f32[16,65536]{1,0:T(8,128)} %get-tuple-element.38.refs_0_, f32[16,8192]{1,0:T(8,128)} %copy-done.4, bf16[24,96]{1,0:T(8,128)(2,1)S(1)} %slice.5.refs_2_), custom_call_target="tpu_custom_call" | custom-call | tf_op jit(solution)/shard_map/cond/branch_1_fun/pallas_call | solution.py:390
  8.2 0.0 copy-done.2
  8.2 1.0 %branch_1_fun.7 = (f32[16,8192]{1,0:T(8,128)S(1)}, f32[16,8192]{1,0:T(8,128)S(1)}, f32[16,8192]{1,0:T(8,128)}) custom-call(f32[16,65536]{1,0:T(8,128)S(1)} %copy-done.2, f32[24,8192]{1,0:T(8,128)S(1)} %branch_1_fun.6.refs_1_), custom_call_target="tpu_custom_call" | custom-call | tf_op jit(solution)/shard_map/cond/branch_1_fun/pallas_call | solution.py:377
  9.2 0.5 collective-permute-start.10
  9.8 0.1 collective-permute-start.7
  9.8 4.0 %collective-permute-start.9 = (f32[24,8192]{1,0:T(8,128)S(1)}, f32[24,8192]{1,0:T(8,128)S(1)}, u32[]{:S(2)}, u32[]{:S(2)}) collective-permute-start(f32[24,8192]{1,0:T(8,128)S(1)} %branch_1_fun.6.refs_1_), channel_id=1, source_target_pairs={{0,4},{1,5},{2,6},{3,7},{4,0},{5,1},{6,2},{7,3},{8,12},{9,13},{10,... | collective-permute-start | bytes 2359304 | tf_op jit(solution)/shard_map/cond/branch_1_fun/ppermute | solution.py:408
  13.8 0.0 collective-permute-done.10.refs_1_
  13.8 1.7 %branch_1_fun.10 = f32[24,8192]{1,0:T(8,128)} custom-call(f32[16,65536]{1,0:T(8,128)S(1)} %copy-done.2, f32[16,8192]{1,0:T(8,128)S(1)} %collective-permute-done.10.refs_1_, bf16[24,96]{1,0:T(8,128)(2,1)S(1)} %slice.5.refs_2_), custom_call_target="tpu_custom_call" | custom-call | tf_op jit(solution)/shard_map/cond/branch_1_fun/pallas_call | solution.py:390
  15.5 1.7 %collective-permute-start.11 = (f32[24,8192]{1,0:T(8,128)}, f32[24,8192]{1,0:T(8,128)S(1)}, u32[]{:S(2)}, u32[]{:S(2)}) collective-permute-start(f32[24,8192]{1,0:T(8,128)} %branch_1_fun.10), channel_id=1, source_target_pairs={{0,6},{1,7},{2,0},{3,1},{4,2},{5,3},{6,4},{7,5},{8,14},{9,15},{10,... | collective-permute-start | bytes 2359304 | tf_op jit(solution)/shard_map/cond/branch_1_fun/ppermute | solution.py:408
  17.2 0.0 collective-permute-done.7.refs_1_
  17.2 1.7 %branch_1_fun.9 = f32[24,8192]{1,0:T(8,128)} custom-call(f32[16,65536]{1,0:T(8,128)S(1)} %copy-done.2, f32[16,8192]{1,0:T(8,128)S(1)} %collective-permute-done.7.refs_1_, bf16[24,96]{1,0:T(8,128)(2,1)S(1)} %slice.5.refs_2_), custom_call_target="tpu_custom_call" | custom-call | tf_op jit(solution)/shard_map/cond/branch_1_fun/pallas_call | solution.py:390
  18.9 0.5 collective-permute-start.8
  19.4 0.0 collective-permute-start.6
  19.4 0.1 fusion.4
  19.5 0.1 tile.16.refs_4_
  19.6 2.0 %collective-permute-done.6.refs_1_ = f32[16,8192]{1,0:T(8,128)} collective-permute-done((f32[16,8192]{1,0:T(8,128)}, f32[16,8192]{1,0:T(8,128)}, u32[]{:S(2)}, u32[]{:S(2)}) %collective-permute-start.6) | collective-permute-done | bytes 524320 | tf_op jit(solution)/shard_map/cond/branch_1_fun/ppermute | solution.py:385
  21.6 2.9 %branch_1_fun.8.refs_0_ = f32[24,8192]{1,0:T(8,128)S(1)} custom-call(f32[16,65536]{1,0:T(8,128)} %get-tuple-element.38.refs_0_, f32[16,8192]{1,0:T(8,128)} %collective-permute-done.6.refs_1_, bf16[24,96]{1,0:T(8,128)(2,1)S(1)} %slice.5.refs_2_), custom_call_target="tpu_custom_call" | custom-call | tf_op jit(solution)/shard_map/cond/branch_1_fun/pallas_call | solution.py:390
  24.5 7.7 %collective-permute-done.9.refs_2_ = f32[24,8192]{1,0:T(8,128)S(1)} collective-permute-done((f32[24,8192]{1,0:T(8,128)S(1)}, f32[24,8192]{1,0:T(8,128)S(1)}, u32[]{:S(2)}, u32[]{:S(2)}) %collective-permute-start.9) | collective-permute-done | bytes 786464 | tf_op jit(solution)/shard_map/cond/branch_1_fun/ppermute | solution.py:408
  32.2 17.3 %collective-permute-done.11.refs_3_ = f32[24,8192]{1,0:T(8,128)S(1)} collective-permute-done((f32[24,8192]{1,0:T(8,128)}, f32[24,8192]{1,0:T(8,128)S(1)}, u32[]{:S(2)}, u32[]{:S(2)}) %collective-permute-start.11) | collective-permute-done | bytes 786464 | tf_op jit(solution)/shard_map/cond/branch_1_fun/ppermute | solution.py:408
  49.6 0.0 collective-permute-done.8.refs_1_
  49.6 5.7 %branch_1_fun.11 = (f32[64,8192]{1,0:T(8,128)}, f32[8,40,128]{2,1,0:T(8,128)S(1)}) custom-call(f32[24,8192]{1,0:T(8,128)S(1)} %branch_1_fun.8.refs_0_, f32[24,8192]{1,0:T(8,128)S(1)} %collective-permute-done.8.refs_1_, f32[24,8192]{1,0:T(8,128)S(1)} %collective-permute-done.9.refs_2_, f32[24,8192]{1,0:T(8,128)S(1)} %collective-permute-done.11.refs_3_, ...), custom_call_target="tpu_custom_call" | custom-call | tf_op jit(solution)/shard_map/cond/branch_1_fun/pallas_call | solution.py:420
  55.3 10.3 %all_to_all.10.in_ref = f32[8,40,128]{2,1,0:T(8,128)} all-to-all(f32[8,40,128]{2,1,0:T(8,128)S(1)} %get-tuple-element.60), channel_id=1, replica_groups=mesh['rows'=16,'store'=8] {'store'}, dimensions={0} | all-to-all | bytes 327680 | tf_op jit(solution)/shard_map/all_to_all | solution.py:449
  65.6 1.8 %shard_map.42 = f32[16,40,128]{2,1,0:T(8,128)} custom-call(f32[8,40,128]{2,1,0:T(8,128)} %all_to_all.10.in_ref), custom_call_target="tpu_custom_call" | custom-call | tf_op jit(solution)/shard_map/pallas_call | solution.py:450
  67.3 16.1 %all_to_all.11.refs_0_ = f32[16,40,128]{2,1,0:T(8,128)} all-to-all(f32[16,40,128]{2,1,0:T(8,128)} %shard_map.42), channel_id=1, replica_groups=mesh['rows'=16,'store'=8] {'rows'}, dimensions={0} | all-to-all | bytes 655360 | tf_op jit(solution)/shard_map/all_to_all | solution.py:451
  83.4 7.5 %shard_map.43 = (f32[64,64]{1,0:T(8,128)}, f32[64,64]{1,0:T(8,128)}) custom-call(f32[16,40,128]{2,1,0:T(8,128)} %all_to_all.11.refs_0_), custom_call_target="tpu_custom_call" | custom-call | tf_op jit(solution)/shard_map/pallas_call | solution.py:452
  90.9 0.0 copy-start
  90.9 0.8 copy-done
  91.7 4.5 %shard_map.44 = f32[64,8192]{1,0:T(8,128)} custom-call(f32[64,64]{1,0:T(8,128)S(1)} %copy-done, f32[64,8192]{1,0:T(8,128)} %get-tuple-element.62.panel_ref), custom_call_target="tpu_custom_call" | custom-call | tf_op jit(solution)/shard_map/pallas_call | solution.py:457
  (8 shorter events, 0.1 us)
Async XLA Ops:
  0.6 1.2 %copy-start.6 = (s32[64]{0:T(128)S(1)}, s32[64]{0:T(128)}, u32[]{:S(2)}) copy-start(s32[64]{0:T(128)} %param.6) | copy-start | bytes 772
  1.7 2.4 %collective-permute-start.18 = (f32[16,8192]{1,0:T(8,128)S(1)}, f32[16,8192]{1,0:T(8,128)S(1)}, u32[]{:S(2)}, u32[]{:S(2)}) collective-permute-start(f32[16,8192]{1,0:T(8,128)S(1)} %shard_map.41), channel_id=1, source_target_pairs={{0,1},{1,0},{2,3},{3,2},{4,5},{5,4},{6,7},{7,6},{8,9},{9,8},{10,11... | collective-permute-start | bytes 1572872 | tf_op jit(solution)/shard_map/ppermute | solution.py:385
  4.2 0.8 copy-start.4
  5.0 3.2 %copy-start.2 = (f32[16,65536]{1,0:T(8,128)S(1)}, f32[16,65536]{1,0:T(8,128)}, u32[]{:S(2)}) copy-start(f32[16,65536]{1,0:T(8,128)} %get-tuple-element.38.refs_0_) | copy-start | bytes 12582916 | tf_op jit(solution)/shard_map/cond
  9.2 4.6 %collective-permute-start.10 = (f32[16,8192]{1,0:T(8,128)S(1)}, f32[16,8192]{1,0:T(8,128)S(1)}, u32[]{:S(2)}, u32[]{:S(2)}) collective-permute-start(f32[16,8192]{1,0:T(8,128)S(1)} %get-tuple-element.43), channel_id=1, source_target_pairs={{0,1},{1,0},{2,3},{3,2},{4,5},{5,4},{6,7},{7,6},{8,9},{9,8},{10,11... | collective-permute-start | bytes 1572872 | tf_op jit(solution)/shard_map/cond/branch_1_fun/ppermute | solution.py:385
  9.8 7.4 %collective-permute-start.7 = (f32[16,8192]{1,0:T(8,128)S(1)}, f32[16,8192]{1,0:T(8,128)S(1)}, u32[]{:S(2)}, u32[]{:S(2)}) collective-permute-start(f32[16,8192]{1,0:T(8,128)S(1)} %get-tuple-element.42), channel_id=1, source_target_pairs={{0,1},{1,0},{2,3},{3,2},{4,5},{5,4},{6,7},{7,6},{8,9},{9,8},{10,11... | collective-permute-start | bytes 1572872 | tf_op jit(solution)/shard_map/cond/branch_1_fun/ppermute | solution.py:385
  9.8 22.4 %collective-permute-start.9 = (f32[24,8192]{1,0:T(8,128)S(1)}, f32[24,8192]{1,0:T(8,128)S(1)}, u32[]{:S(2)}, u32[]{:S(2)}) collective-permute-start(f32[24,8192]{1,0:T(8,128)S(1)} %branch_1_fun.6.refs_1_), channel_id=1, source_target_pairs={{0,4},{1,5},{2,6},{3,7},{4,0},{5,1},{6,2},{7,3},{8,12},{9,13},{10,... | collective-permute-start | bytes 2359304 | tf_op jit(solution)/shard_map/cond/branch_1_fun/ppermute | solution.py:408
  15.5 34.1 %collective-permute-start.11 = (f32[24,8192]{1,0:T(8,128)}, f32[24,8192]{1,0:T(8,128)S(1)}, u32[]{:S(2)}, u32[]{:S(2)}) collective-permute-start(f32[24,8192]{1,0:T(8,128)} %branch_1_fun.10), channel_id=1, source_target_pairs={{0,6},{1,7},{2,0},{3,1},{4,2},{5,3},{6,4},{7,5},{8,14},{9,15},{10,... | collective-permute-start | bytes 2359304 | tf_op jit(solution)/shard_map/cond/branch_1_fun/ppermute | solution.py:408
  18.9 30.7 %collective-permute-start.8 = (f32[24,8192]{1,0:T(8,128)}, f32[24,8192]{1,0:T(8,128)S(1)}, u32[]{:S(2)}, u32[]{:S(2)}) collective-permute-start(f32[24,8192]{1,0:T(8,128)} %branch_1_fun.9), channel_id=1, source_target_pairs={{0,2},{1,3},{2,4},{3,5},{4,6},{5,7},{6,0},{7,1},{8,10},{9,11},{10,... | collective-permute-start | bytes 2359304 | tf_op jit(solution)/shard_map/cond/branch_1_fun/ppermute | solution.py:408
  19.4 2.3 %collective-permute-start.6 = (f32[16,8192]{1,0:T(8,128)}, f32[16,8192]{1,0:T(8,128)}, u32[]{:S(2)}, u32[]{:S(2)}) collective-permute-start(f32[16,8192]{1,0:T(8,128)} %get-tuple-element.41), channel_id=1, source_target_pairs={{0,1},{1,0},{2,3},{3,2},{4,5},{5,4},{6,7},{7,6},{8,9},{9,8},{10,11... | collective-permute-start | bytes 1572872 | tf_op jit(solution)/shard_map/cond/branch_1_fun/ppermute | solution.py:385
  90.9 0.8 copy-start
